TPU v7x, 1024 devices: a whole 4x4x32 slice. The times are simulated.
1024 devices in a mesh: fsdp: 128 (over z, x), tensor: 8 (over y, core).
Axes of the slice: x: 4, y: 4, z: 32, core: 2. Of those that a mesh axis runs over, the one named last changes fastest.
Arguments:
- momentum: bfloat16 [16384, 26624], P('fsdp', 'tensor'), may hold values from -6 to 6
- gradient: bfloat16 [16384, 26624], P('fsdp', 'tensor')
- basis: float32 [26624, 128], P(('tensor', 'fsdp')), may hold values from -0.0390625 to 0.0390625
Outputs:
- update: bfloat16 [16384, 26624], P('fsdp', 'tensor')
- new_momentum: bfloat16 [16384, 26624], P('fsdp', 'tensor')
All inputs are finite; a program needn't handle non-finite values.
Results may differ from a plain program's by a relative error of at most 0.007.
The roundings to bfloat16 on the way count: a program that leaves them out, or rounds other values in their place, can miss the bound.
Values may be sent and summed in bfloat16 or wider, within the bound.
A program may use at most 32 MiB of HBM per device.

v0:
```python
import math

import jax
import jax.numpy as jnp
from jax import lax
from jax.sharding import PartitionSpec as P

D = 16384
FF = 26624
RANK = 128


def orthonormal(panel, gram):
    factor = jnp.linalg.cholesky(gram)
    return lax.linalg.triangular_solve(
        factor, panel, left_side=False, lower=True, transpose_a=True
    ).astype(jnp.bfloat16)


def gram_local(panel):
    return jnp.dot(
        panel.T, panel, precision=lax.Precision.HIGHEST, preferred_element_type=jnp.float32
    )


def body(momentum, gradient, basis):
    summed = momentum.astype(jnp.float32) + gradient.astype(jnp.float32)
    summed_b = summed.astype(jnp.bfloat16)
    scale = math.sqrt(D * FF / RANK)
    block = summed_b
    partial_value = jnp.dot(
        block,
        lax.all_gather(basis.astype(jnp.bfloat16), "fsdp", axis=0, tiled=True),
        preferred_element_type=jnp.float32,
    )
    panel = lax.psum(partial_value, "tensor")
    gram = lax.psum(gram_local(panel), "fsdp")
    ortho = orthonormal(panel, gram)
    block = summed_b
    cross_shard = lax.psum_scatter(
        lax.dot_general(block, ortho, (((0,), (0,)), ((), ())), preferred_element_type=jnp.float32),
        "fsdp",
        scatter_dimension=0,
        tiled=True,
    )
    colsq = lax.psum(jnp.sum(cross_shard * cross_shard, axis=0), ("fsdp", "tensor"))
    scaleinv = 1.0 / jnp.sqrt(colsq + 1e-06)
    piece = lax.all_gather(cross_shard.astype(jnp.bfloat16), "fsdp", axis=0, tiled=True)
    block = summed
    newbasis = (piece.astype(jnp.float32) * scaleinv).astype(jnp.bfloat16)
    upd = scale * lax.dot_general(
        ortho, newbasis, (((1,), (1,)), ((), ())), preferred_element_type=jnp.float32
    )
    mom = block - 0.05 * lax.dot_general(
        ortho, piece, (((1,), (1,)), ((), ())), preferred_element_type=jnp.float32
    )
    both = jnp.stack([upd, mom])
    return (both[0].astype(jnp.bfloat16), both[1].astype(jnp.bfloat16))


def solution(mesh):
    in_specs = (P("fsdp", "tensor"), P("fsdp", "tensor"), P(("tensor", "fsdp"), None))
    out_specs = (P("fsdp", "tensor"), P("fsdp", "tensor"))
    return jax.shard_map(body, mesh=mesh, in_specs=in_specs, out_specs=out_specs, check_vma=False)
```

profile of v0, /device:TPU:2, one launch (start us, length us, event | category | flops | bytes accessed | tf_op | source)
XLA Modules:
  0.0 1599.4 jit_solution(13944611273096443094)
XLA Ops:
  8.1 214.1 %all-gather = bf16[128,26,128]{2,1,0:T(8,128)(2,1)S(1)} all-gather(bf16[1,26,128]{2,1,0:T(8,128)(2,1)S(1)} %convert_bitcast_fusion), channel_id=1, replica_groups=mesh['fsdp'=128,'tensor'=8] {'fsdp'}, dimensions={0}, use_global_device_ids=true | all-gather | bytes 858624 | tf_op jit(solution)/shard_map/all_gather | solution.py:33
  225.6 86.8 %all-reduce.5.cloned.1.call-done = f32[128,128]{1,0:T(8,128)} async-done(((f32[128,128]{1,0:T(8,128)}), f32[128,128]{1,0:T(8,128)}) %all-reduce.5.cloned.1.call-update) | async-done | bytes 65552 | tf_op jit(solution)/shard_map/psum | solution.py:36
  314.2 493.0 %all-reduce.7.cloned.1.call-done = f32[128,128]{0,1:T(8,128)} async-done(((f32[128,128]{0,1:T(8,128)}), f32[128,128]{0,1:T(8,128)}) %all-reduce.7.cloned.1.call-update) | async-done | bytes 65552 | tf_op jit(solution)/shard_map/psum | solution.py:37
  809.0 11.7 cholesky.16
  822.0 9.8 custom-call.6
  833.3 286.3 %fusion = f32[32,128]{1,0:T(8,128)S(1)} fusion(f32[3328,128]{1,0:T(8,128)S(1)} %fusion.6), kind=kCustom, calls=%all-reduce-scatter | all-reduce-scatter fusion | flops 524289 | bytes 1724416
  1120.9 2.8 collective-permute-start.21
  1123.7 3.3 collective-permute-start.20
  1127.0 5.5 collective-permute-start.23
  1132.5 12.2 collective-permute-start.19
  1146.0 10.4 collective-permute-start.17
  1156.5 3.4 collective-permute-start.16
  1159.8 7.1 collective-permute-start.15
  1167.0 2.9 collective-permute-start.14
  1169.9 6.6 collective-permute-start.13
  1182.4 3.8 collective-permute-start.9
  1188.8 5.1 collective-permute-start.7
  1195.2 3.7 collective-permute-start.5
  1198.9 3.4 collective-permute-start.4
  1207.1 3.4 collective-permute-start.1
  1210.5 3.9 collective-permute-start
  1216.3 3.1 concatenate
  1219.5 152.1 %psum.23 = f32[128]{0:T(128)S(1)} all-reduce(f32[128]{0:T(128)S(1)} %multiply_reduce_fusion), channel_id=1, replica_groups=mesh['fsdp'=128,'tensor'=8] {'fsdp','tensor'}, use_global_device_ids=true, to_apply=%region_6.7 | all-reduce | flops 128 | bytes 1024 | tf_op jit(solution)/shard_map/psum | solution.py:46
  1371.6 217.0 %all-gather.1 = bf16[128,26,128]{2,1,0:T(8,128)(2,1)} all-gather(bf16[1,26,128]{2,1,0:T(8,128)(2,1)S(1)} %fusion.13), channel_id=1, replica_groups=mesh['fsdp'=128,'tensor'=8] {'fsdp'}, dimensions={0}, use_global_device_ids=true | all-gather | bytes 858624 | tf_op jit(solution)/shard_map/all_gather | solution.py:48
  (60 shorter events, 33.0 us)
Async XLA Ops:
  7.2 305.2 %all-reduce.5.cloned.1.call-start = ((), (), s32[]{:S(2)}) async-start(), calls=%async_computation | async-start | bytes 131072 | tf_op jit(solution)/shard_map/psum | solution.py:36
  225.5 581.7 %all-reduce.7.cloned.1.call-start = ((), (), s32[]{:S(2)}) async-start(), calls=%async_computation.1 | async-start | bytes 131072 | tf_op jit(solution)/shard_map/psum | solution.py:37
  1119.6 26.4 %collective-permute-start.22 = (f32[32,128]{1,0:T(8,128)S(1)}, f32[32,128]{1,0:T(8,128)S(1)}, u32[]{:S(2)}, u32[]{:S(2)}) collective-permute-start(f32[32,128]{1,0:T(8,128)S(1)} %fusion), channel_id=1, source_target_pairs={{0,184},{8,192},{16,200},{24,208},{32,216},{40,224},{48,232},{56,2... | collective-permute-start | bytes 49160
  1120.9 35.6 %collective-permute-start.21 = (f32[32,128]{1,0:T(8,128)S(1)}, f32[32,128]{1,0:T(8,128)S(1)}, u32[]{:S(2)}, u32[]{:S(2)}) collective-permute-start(f32[32,128]{1,0:T(8,128)S(1)} %fusion), channel_id=1, source_target_pairs={{0,176},{8,184},{16,192},{24,200},{32,208},{40,216},{48,224},{56,2... | collective-permute-start | bytes 49160
  1123.7 36.2 %collective-permute-start.20 = (f32[32,128]{1,0:T(8,128)S(1)}, f32[32,128]{1,0:T(8,128)S(1)}, u32[]{:S(2)}, u32[]{:S(2)}) collective-permute-start(f32[32,128]{1,0:T(8,128)S(1)} %fusion), channel_id=1, source_target_pairs={{0,168},{8,176},{16,184},{24,192},{32,200},{40,208},{48,216},{56,2... | collective-permute-start | bytes 49160
  1127.0 17.7 %collective-permute-start.23 = (f32[26,128]{1,0:T(8,128)S(1)}, f32[26,128]{1,0:T(8,128)S(1)}, u32[]{:S(2)}, u32[]{:S(2)}) collective-permute-start(f32[26,128]{1,0:T(8,128)S(1)} %slice.10), channel_id=1, source_target_pairs={{0,192},{8,200},{16,208},{24,216},{32,224},{40,232},{48,240},{56,2... | collective-permute-start | bytes 39944
  1132.5 34.5 %collective-permute-start.19 = (f32[32,128]{1,0:T(8,128)S(1)}, f32[32,128]{1,0:T(8,128)S(1)}, u32[]{:S(2)}, u32[]{:S(2)}) collective-permute-start(f32[32,128]{1,0:T(8,128)S(1)} %fusion), channel_id=1, source_target_pairs={{0,160},{8,168},{16,176},{24,184},{32,192},{40,200},{48,208},{56,2... | collective-permute-start | bytes 49160
  1144.7 25.2 %collective-permute-start.18 = (f32[32,128]{1,0:T(8,128)S(1)}, f32[32,128]{1,0:T(8,128)S(1)}, u32[]{:S(2)}, u32[]{:S(2)}) collective-permute-start(f32[32,128]{1,0:T(8,128)S(1)} %fusion), channel_id=1, source_target_pairs={{0,152},{8,160},{16,168},{24,176},{32,184},{40,192},{48,200},{56,2... | collective-permute-start | bytes 49160
  1146.0 30.4 %collective-permute-start.17 = (f32[32,128]{1,0:T(8,128)S(1)}, f32[32,128]{1,0:T(8,128)S(1)}, u32[]{:S(2)}, u32[]{:S(2)}) collective-permute-start(f32[32,128]{1,0:T(8,128)S(1)} %fusion), channel_id=1, source_target_pairs={{0,144},{8,152},{16,160},{24,168},{32,176},{40,184},{48,192},{56,2... | collective-permute-start | bytes 49160
  1156.5 21.3 %collective-permute-start.16 = (f32[32,128]{1,0:T(8,128)S(1)}, f32[32,128]{1,0:T(8,128)S(1)}, u32[]{:S(2)}, u32[]{:S(2)}) collective-permute-start(f32[32,128]{1,0:T(8,128)S(1)} %fusion), channel_id=1, source_target_pairs={{0,136},{8,144},{16,152},{24,160},{32,168},{40,176},{48,184},{56,1... | collective-permute-start | bytes 49160
  1159.8 20.4 %collective-permute-start.15 = (f32[32,128]{1,0:T(8,128)S(1)}, f32[32,128]{1,0:T(8,128)S(1)}, u32[]{:S(2)}, u32[]{:S(2)}) collective-permute-start(f32[32,128]{1,0:T(8,128)S(1)} %fusion), channel_id=1, source_target_pairs={{0,128},{8,136},{16,144},{24,152},{32,160},{40,168},{48,176},{56,1... | collective-permute-start | bytes 49160
  1167.0 15.4 collective-permute-start.14
  1169.9 16.4 %collective-permute-start.13 = (f32[32,128]{1,0:T(8,128)S(1)}, f32[32,128]{1,0:T(8,128)S(1)}, u32[]{:S(2)}, u32[]{:S(2)}) collective-permute-start(f32[32,128]{1,0:T(8,128)S(1)} %fusion), channel_id=1, source_target_pairs={{0,112},{8,120},{16,128},{24,136},{32,144},{40,152},{48,160},{56,1... | collective-permute-start | bytes 49160
  1176.5 12.3 collective-permute-start.12
  1177.8 16.1 %collective-permute-start.11 = (f32[32,128]{1,0:T(8,128)S(1)}, f32[32,128]{1,0:T(8,128)S(1)}, u32[]{:S(2)}, u32[]{:S(2)}) collective-permute-start(f32[32,128]{1,0:T(8,128)S(1)} %fusion), channel_id=1, source_target_pairs={{0,96},{8,104},{16,112},{24,120},{32,128},{40,136},{48,144},{56,15... | collective-permute-start | bytes 49160
  1180.3 14.9 collective-permute-start.10
  1182.4 16.5 %collective-permute-start.9 = (f32[32,128]{1,0:T(8,128)S(1)}, f32[32,128]{1,0:T(8,128)S(1)}, u32[]{:S(2)}, u32[]{:S(2)}) collective-permute-start(f32[32,128]{1,0:T(8,128)S(1)} %fusion), channel_id=1, source_target_pairs={{0,80},{8,88},{16,96},{24,104},{32,112},{40,120},{48,128},{56,136}... | collective-permute-start | bytes 49160
  1186.3 16.1 %collective-permute-start.8 = (f32[32,128]{1,0:T(8,128)S(1)}, f32[32,128]{1,0:T(8,128)S(1)}, u32[]{:S(2)}, u32[]{:S(2)}) collective-permute-start(f32[32,128]{1,0:T(8,128)S(1)} %fusion), channel_id=1, source_target_pairs={{0,72},{8,80},{16,88},{24,96},{32,104},{40,112},{48,120},{56,128},... | collective-permute-start | bytes 49160
  1188.8 16.1 %collective-permute-start.7 = (f32[32,128]{1,0:T(8,128)S(1)}, f32[32,128]{1,0:T(8,128)S(1)}, u32[]{:S(2)}, u32[]{:S(2)}) collective-permute-start(f32[32,128]{1,0:T(8,128)S(1)} %fusion), channel_id=1, source_target_pairs={{0,64},{8,72},{16,80},{24,88},{32,96},{40,104},{48,112},{56,120},{... | collective-permute-start | bytes 49160
  1193.9 13.2 collective-permute-start.6
  1195.2 15.3 collective-permute-start.5
  1198.9 17.4 %collective-permute-start.4 = (f32[32,128]{1,0:T(8,128)S(1)}, f32[32,128]{1,0:T(8,128)S(1)}, u32[]{:S(2)}, u32[]{:S(2)}) collective-permute-start(f32[32,128]{1,0:T(8,128)S(1)} %fusion), channel_id=1, source_target_pairs={{0,40},{8,48},{16,56},{24,64},{32,72},{40,80},{48,88},{56,96},{64,... | collective-permute-start | bytes 49160
  1202.3 13.9 collective-permute-start.3
  1204.8 11.5 collective-permute-start.2
  (4 other events, 447.4 us)
Sparse Core Ops, SparseCore 0:
  225.6 86.6 all-reduce.4
  316.8 490.3 all-reduce.6
where the time goes:
time: 1600 us
  blocking collectives  869 us (54%)
  waiting for transfers between devices  580 us (36%)
  starting transfers between devices  94.4 us (6%)
  other arithmetic  24.6 us (2%)
    psum x1, waiting for transfers between devices, body(): gram = lax.psum(gram_local(panel), 'fsdp')  493 us
    unnamed x1, blocking collectives  286 us
    all_gather x1, blocking collectives, body(): lax.all_gather(cross_shard.astype(jnp.bfloat16), 'fsdp', axis=0, tiled=True)  217 us
    all_gather x1, blocking collectives, body(): lax.all_gather(basis.astype(jnp.bfloat16), 'fsdp', axis=0, tiled=True)  214 us
    psum x1, blocking collectives, body(): lax.psum(jnp.sum(cross_shard * cross_shard, axis=0), ('fsdp', 'tensor'))  152 us
    unnamed x24, starting transfers between devices  94.4 us
    psum x1, waiting for transfers between devices, body(): panel = lax.psum(partial_value, 'tensor')  86.8 us
  transfers between devices with their start and end apart: 26, of which 2 were waited for; matrix products, arithmetic and copies ran while one was open for 0% of the time, Pallas kernels for 0%

commit v1 on v0

v1 whole, which is shorter than its diff:
```python
import functools
import math

import jax
import jax.numpy as jnp
from jax import lax
from jax.experimental import pallas as pl
from jax.experimental.pallas import tpu as pltpu
from jax.sharding import PartitionSpec as P

MESH = pl.DeviceIdType.MESH
HIGHEST = lax.Precision.HIGHEST
RANK = 128
NX = 4
NEAR = 8
FAR = 4
F32 = jnp.float32
BF16 = jnp.bfloat16


class Plan:
    def __init__(self, n_fsdp, n_tensor, rows, cols):
        self.nz, self.nx, self.nt = n_fsdp // NX, NX, n_tensor
        assert self.nz == NEAR * FAR
        self.rows, self.cols = rows, cols
        self.piece = cols // n_fsdp
        self.slot = -(-self.piece // 16) * 16
        self.block = self.piece * FAR
        self.sent = -(-self.block // 16) * 16
        self.near = [d for d in range(NEAR // 2, 0, -1)] + [-d for d in range((NEAR - 1) // 2, 0, -1)]
        self.near.sort(key=abs)
        self.strip = rows // n_tensor
        self.chunk = 256 if cols % 256 == 0 else cols // self.nx


class Copies:
    def __init__(self, send, recv):
        self.send, self.recv, self.used, self.out = send, recv, 0, []

    def start(self, src, dst, device):
        i = self.used
        self.used += 1
        copy = pltpu.make_async_remote_copy(
            src_ref=src, dst_ref=dst, send_sem=self.send.at[i], recv_sem=self.recv.at[i],
            device_id=device, device_id_type=MESH,
        )
        copy.start()
        self.out.append(copy)
        return copy

    def finish(self):
        for copy in self.out:
            copy.wait_send()


def n_copies(plan):
    near, far, x, t = len(plan.near), FAR - 1, plan.nx - 1, plan.nt - 1
    gather = far + near + NEAR * x
    total = gather + 2 * t + (near + far + x + t) + (NEAR * x + near + far) + gather + (near + far + x + t)
    return max(total, 1)


def factor(gp_ref, ot_ref):
    n = RANK
    lane = lax.broadcasted_iota(jnp.int32, (n, n), 1)
    lane1 = lax.broadcasted_iota(jnp.int32, (1, n), 1)
    row1 = lax.broadcasted_iota(jnp.int32, (n, 1), 0)

    def step(s, carry):
        j = s * 4
        gram = gp_ref[:, :n]
        cols, rows = [], []
        for p in range(4):
            rows.append(gp_ref[pl.ds(j + p, 1), :])
            cols.append(jnp.sum(jnp.where(lane == j + p, gram, 0.0), axis=1, keepdims=True))
        a = [[jnp.sum(jnp.where(lane1 == j + q, rows[p][:, :n], 0.0), axis=1, keepdims=True)
              for q in range(p + 1)] for p in range(4)]
        inv, mults = [], []
        for p in range(4):
            for q in range(p):
                low = a[p][q] * inv[q]
                rows[p] = rows[p] - low * rows[q]
                cols[p] = cols[p] - low * cols[q]
                for r in range(p, 4):
                    a[r][p] = a[r][p] - low * a[r][q]
            inv.append(1.0 / a[p][p])
            mults.append(jnp.where(row1 > j + 3, cols[p] * inv[p], 0.0))
            ot_ref[pl.ds(j + p, 1), :] = rows[p][:, n:] * (1.0 / jnp.sqrt(a[p][p]))
        new = gp_ref[...]
        for p in range(4):
            new = new - mults[p] * rows[p]
        gp_ref[...] = new
        return carry

    lax.fori_loop(0, n // 4, step, 0)


def kernel(plan, m_ref, g_ref, b_ref, ortho_ref, piece_ref, newb_ref,
           sb, basis_buf, tile, basis32, part, part_in, strip, panel, gram, gram_x, gram_n, gram_f, gram_t,
           strip_x, strip_n, strip_f, gp, ot,
           cross, cross_x, sum_x, cross_n, sum_n, cross_f, cross_buf, nat,
           sq, sq_f, sq_n, sq_x, sq_t, send_sem, recv_sem):
    f, t = lax.axis_index("fsdp"), lax.axis_index("tensor")
    nz, nx, nt = plan.nz, plan.nx, plan.nt
    z, x = f // nx, f % nx
    near_id, far_id = z % NEAR, z // NEAR
    comm = Copies(send_sem, recv_sem)

    def at_z(d):
        return (lax.rem(z + d + nz, nz) * nx + x, t)

    def at_x(d):
        return (z * nx + lax.rem(x + d, nx), t)

    def at_t(d):
        return (f, lax.rem(t + d, nt))

    barrier = pltpu.get_barrier_semaphore()
    peers = [at_z(NEAR * d) for d in range(1, FAR)] + [at_z(-d) for d in plan.near]
    peers += [at_x(d) for d in range(1, nx)] + [at_t(d) for d in range(1, nt)]
    for device in peers:
        pl.semaphore_signal(barrier, inc=1, device_id=device, device_id_type=MESH)

    basis_buf[x, near_id, far_id, 0:plan.slot] = jnp.zeros((plan.slot, RANK), BF16)
    basis_buf[x, near_id, far_id, 0:plan.piece] = b_ref[...].astype(BF16)
    chunk = plan.chunk
    n_chunks = plan.cols // chunk

    def add(i, carry):
        c = pl.ds(pl.multiple_of(i * chunk, chunk), chunk)
        sb[:, c] = (m_ref[:, c].astype(F32) + g_ref[:, c].astype(F32)).astype(BF16)
        return carry

    lax.fori_loop(0, n_chunks, add, 0)
    pl.semaphore_wait(barrier, len(peers))

    def spread(buf, view, wait_first=()):
        def forward(near):
            block = view(x, near)
            return [comm.start(block, block, at_x(d)) for d in range(1, nx)]

        block = view(x, near_id)
        zs = [comm.start(block, block, at_z(d)) for d in plan.near]
        return forward, zs

    own = basis_buf.at[x, near_id, far_id]
    for copy in [comm.start(own, own, at_z(NEAR * d)) for d in range(1, FAR)]:
        copy.wait_recv()
    forward, zs = spread(basis_buf, lambda xx, nn: basis_buf.at[xx, nn])
    xs = forward(near_id)
    for d, copy in zip(plan.near, zs):
        copy.wait_recv()
        xs += forward(lax.rem(near_id - d + NEAR, NEAR))
    for copy in xs:
        copy.wait_recv()

    def unpack(zz, carry):
        for xx in range(nx):
            tile[xx * plan.piece:(xx + 1) * plan.piece, :] = basis_buf[
                xx, zz % NEAR, zz // NEAR, 0:plan.piece].astype(F32)
        n = nx * plan.piece
        basis32[pl.ds(pl.multiple_of(zz * n, 8), n), :] = tile[...]
        return carry

    lax.fori_loop(0, nz, unpack, 0)
    part[...] = jnp.zeros_like(part)

    def multiply(i, carry):
        c = pl.ds(pl.multiple_of(i * chunk, chunk), chunk)
        part[...] += jnp.dot(sb[:, c], basis32[c, :].astype(BF16), preferred_element_type=F32)
        return carry

    lax.fori_loop(0, n_chunks, multiply, 0)

    w = plan.strip

    def strip_of(ref, i):
        return ref.at[pl.ds(pl.multiple_of(i * w, w), w)]

    got = [comm.start(strip_of(part, lax.rem(t + d, nt)), part_in.at[d], at_t(d)) for d in range(1, nt)]
    total = strip_of(part, t)[...]
    for d, copy in zip(range(1, nt), got):
        copy.wait_recv()
        total = total + part_in[d]
    strip_of(panel, t)[...] = total
    mine = strip_of(panel, t)
    got = [comm.start(mine, mine, at_t(d)) for d in range(1, nt)]
    for copy in got:
        copy.wait_recv()

    pan = panel[...]
    gram[...] = lax.dot_general(
        pan, pan, (((0,), (0,)), ((), ())), precision=HIGHEST, preferred_element_type=F32)
    strip[...] = strip_of(gram, t)[...]

    def reduce(src, slots, out, devices):
        got = [comm.start(src, slots.at[i], device) for i, device in enumerate(devices)]
        total = src[...]
        for i, copy in enumerate(got):
            copy.wait_recv()
            total = total + slots[i]
        out[...] = total

    x_devices = [at_x(d) for d in range(1, nx)]
    near_devices = [at_z(d) for d in plan.near]
    far_devices = [at_z(NEAR * d) for d in range(1, FAR)]
    reduce(strip, gram_x, strip_x, x_devices)
    reduce(strip_x, gram_n, strip_n, near_devices)
    reduce(strip_n, gram_f, strip_f, far_devices)
    mine = strip_of(gram_t, t)
    mine[...] = strip_f[...]
    got = [comm.start(mine, mine, at_t(d)) for d in range(1, nt)]
    gp[:, RANK:] = pan.T
    for copy in got:
        copy.wait_recv()
    gp[:, :RANK] = gram_t[...]

    factor(gp, ot)
    ortho = ot[...].T.astype(BF16)
    ortho_ref[...] = ortho

    def cross_chunk(i, carry):
        c = pl.ds(pl.multiple_of(i * chunk, chunk), chunk)
        cross[c, :] = lax.dot_general(
            sb[:, c], ortho, (((0,), (0,)), ((), ())), preferred_element_type=F32)
        return carry

    lax.fori_loop(0, n_chunks, cross_chunk, 0)

    block, per_x = plan.block, plan.block * NEAR

    def rows_of(xx, near):
        return pl.ds(pl.multiple_of(xx * per_x + near * block, 8), block)

    order = plan.near[::-1] + [0]
    got = []
    for o, d in enumerate(order):
        near = lax.rem(near_id + d + NEAR, NEAR)
        got.append([comm.start(cross.at[rows_of(lax.rem(x + dx, nx), near)], cross_x.at[dx - 1, o], at_x(dx))
                    for dx in range(1, nx)])
    sum_n[...] = jnp.zeros_like(sum_n)
    zs = []
    for o, d in enumerate(order):
        near = lax.rem(near_id + d + NEAR, NEAR)
        total = cross[rows_of(x, near), :]
        for dx, copy in enumerate(got[o]):
            copy.wait_recv()
            total = total + cross_x[dx, o]
        if d:
            sum_x[o] = total
            zs.append(comm.start(sum_x.at[o], cross_n.at[o], at_z(d)))
        else:
            for i, copy in enumerate(zs):
                copy.wait_recv()
                total = total + cross_n[i]
            sum_n[0:block, :] = total
    slot = plan.slot

    def slot_rows(i):
        return pl.ds(pl.multiple_of(i * slot, slot), slot)

    got = [comm.start(sum_n.at[slot_rows(lax.rem(far_id + d, FAR))], cross_f.at[d - 1], at_z(NEAR * d))
           for d in range(1, FAR)]
    total = sum_n[slot_rows(far_id), :]
    for i, copy in enumerate(got):
        copy.wait_recv()
        total = total + cross_f[i]

    sq[0] = jnp.broadcast_to(jnp.sum(total * total, axis=0, keepdims=True), (8, RANK))
    own = cross_buf.at[x, near_id, slot_rows(far_id)]
    own[...] = total.astype(BF16)
    got = [comm.start(own, own, device) for device in far_devices]
    reduce(sq.at[0], sq_f, sq.at[1], far_devices)
    for copy in got:
        copy.wait_recv()
    forward, zs = spread(cross_buf, lambda xx, nn: cross_buf.at[xx, nn, pl.ds(0, plan.sent)])
    reduce(sq.at[1], sq_n, sq.at[2], near_devices)
    reduce(sq.at[2], sq_x, sq.at[3], x_devices)
    got = [comm.start(sq.at[3], sq_t.at[d - 1], at_t(d)) for d in range(1, nt)]
    xs = forward(near_id)
    for d, copy in zip(plan.near, zs):
        copy.wait_recv()
        xs += forward(lax.rem(near_id - d + NEAR, NEAR))
    total = sq[3]
    for i, copy in enumerate(got):
        copy.wait_recv()
        total = total + sq_t[i]
    scaleinv = 1.0 / jnp.sqrt(total[0:1, :] + 1e-06)
    for copy in xs:
        copy.wait_recv()

    def settle(i, carry):
        nat[pl.ds(pl.multiple_of(i * block, 8), block), :] = cross_buf[
            i // NEAR, i % NEAR, 0:block].astype(F32)
        return carry

    lax.fori_loop(0, nx * NEAR, settle, 0)

    def scale_rows(i, carry):
        c = pl.ds(pl.multiple_of(i * chunk, 16), chunk)
        value = nat[c, :]
        piece_ref[c, :] = value.astype(BF16)
        newb_ref[c, :] = (value * scaleinv).astype(BF16)
        return carry

    lax.fori_loop(0, n_chunks, scale_rows, 0)
    comm.finish()


def exchange(plan, momentum, gradient, basis):
    nx, nt, near, far = plan.nx, plan.nt, max(len(plan.near), 1), FAR - 1
    vmem = pl.BlockSpec(memory_space=pltpu.VMEM)
    w = plan.strip
    scratch = [
        pltpu.VMEM((plan.rows, plan.cols), BF16),
        pltpu.VMEM((nx, NEAR, FAR, plan.slot, RANK), BF16),
        pltpu.VMEM((nx * plan.piece, RANK), F32),
        pltpu.VMEM((plan.cols, RANK), F32),
        pltpu.VMEM((plan.rows, RANK), F32),
        pltpu.VMEM((nt, w, RANK), F32),
        pltpu.VMEM((w, RANK), F32),
        pltpu.VMEM((plan.rows, RANK), F32),
        pltpu.VMEM((RANK, RANK), F32),
        pltpu.VMEM((nx - 1, w, RANK), F32),
        pltpu.VMEM((near, w, RANK), F32),
        pltpu.VMEM((far, w, RANK), F32),
        pltpu.VMEM((RANK, RANK), F32),
        pltpu.VMEM((w, RANK), F32),
        pltpu.VMEM((w, RANK), F32),
        pltpu.VMEM((w, RANK), F32),
        pltpu.VMEM((RANK, RANK + plan.rows), F32),
        pltpu.VMEM((RANK, plan.rows), F32),
        pltpu.VMEM((plan.cols, RANK), F32),
        pltpu.VMEM((nx - 1, NEAR, plan.block, RANK), F32),
        pltpu.VMEM((near, plan.block, RANK), F32),
        pltpu.VMEM((near, plan.block, RANK), F32),
        pltpu.VMEM((FAR * plan.slot, RANK), F32),
        pltpu.VMEM((far, plan.slot, RANK), F32),
        pltpu.VMEM((nx, NEAR, FAR * plan.slot, RANK), BF16),
        pltpu.VMEM((plan.cols, RANK), F32),
        pltpu.VMEM((4, 8, RANK), F32),
        pltpu.VMEM((far, 8, RANK), F32),
        pltpu.VMEM((near, 8, RANK), F32),
        pltpu.VMEM((nx - 1, 8, RANK), F32),
        pltpu.VMEM((max(nt - 1, 1), 8, RANK), F32),
        pltpu.SemaphoreType.DMA((n_copies(plan),)),
        pltpu.SemaphoreType.DMA((n_copies(plan),)),
    ]
    return pl.pallas_call(
        functools.partial(kernel, plan),
        out_shape=(
            jax.ShapeDtypeStruct((plan.rows, RANK), BF16),
            jax.ShapeDtypeStruct((plan.cols, RANK), BF16),
            jax.ShapeDtypeStruct((plan.cols, RANK), BF16),
        ),
        in_specs=[vmem] * 3,
        out_specs=(vmem,) * 3,
        scratch_shapes=scratch,
        compiler_params=pltpu.CompilerParams(
            collective_id=0, has_side_effects=True, vmem_limit_bytes=48 * 1024 * 1024),
        cost_estimate=pl.CostEstimate(
            flops=4 * plan.rows * plan.cols * RANK, bytes_accessed=6 * plan.rows * plan.cols, transcendentals=0),
        name="dion_exchange",
    )(momentum, gradient, basis)


def solution(mesh):
    n_fsdp, n_tensor = mesh.shape["fsdp"], mesh.shape["tensor"]

    def body(momentum, gradient, basis):
        rows, cols = momentum.shape
        plan = Plan(n_fsdp, n_tensor, rows, cols)
        scale = math.sqrt(rows * n_fsdp * cols * n_tensor / RANK)
        ortho, piece, newbasis = exchange(plan, momentum, gradient, basis)
        dims = (((1,), (1,)), ((), ()))
        update = scale * lax.dot_general(ortho, newbasis, dims, preferred_element_type=F32)
        summed = momentum.astype(F32) + gradient.astype(F32)
        moved = summed - 0.05 * lax.dot_general(ortho, piece, dims, preferred_element_type=F32)
        return update.astype(BF16), moved.astype(BF16)

    in_specs = (P("fsdp", "tensor"), P("fsdp", "tensor"), P(("tensor", "fsdp"), None))
    out_specs = (P("fsdp", "tensor"), P("fsdp", "tensor"))
    return jax.shard_map(body, mesh=mesh, in_specs=in_specs, out_specs=out_specs, check_vma=False)
```

time: 1600 us -> 177 us (0.11)
  the two profiles are of different devices: /device:TPU:2 before, /device:TPU:1 now
where the time goes in v1:
time: 177 us; the launch traced here: 176 us
  Pallas kernels  170 us (96%)
  local copies, waits for them, and re-layouts  3.02 us (2%)
  matrix products  2.61 us (1%)
    pallas_call x1, Pallas kernels, exchange(): pl.pallas_call(functools.partial(kernel, plan), out_shape=(jax.ShapeDtype...  170 us

profile of v1, /device:TPU:1, one launch (start us, length us, event | category | flops | bytes accessed | tf_op | source)
XLA Modules:
  0.0 176.0 jit_solution(795552583595343964)
XLA Ops:
  0.6 0.0 copy-start
  0.6 1.1 copy-done
  1.8 0.0 copy-start.1
  1.8 1.2 copy-done.1
  2.9 0.0 copy-start.2
  2.9 0.7 copy-done.2
  3.7 169.7 %dion_exchange.1 = (bf16[128,128]{1,0:T(8,128)(2,1)S(1)}, bf16[3328,128]{1,0:T(8,128)(2,1)S(1)}, bf16[3328,128]{1,0:T(8,128)(2,1)S(1)}) custom-call(bf16[128,3328]{1,0:T(8,128)(2,1)S(1)} %copy-done, bf16[128,3328]{1,0:T(8,128)(2,1)S(1)} %copy-done.1, f32[26,128]{1,0:T(8,128)S(1)} %copy-done.2), custom_call_target="tpu_custom_call" | custom-call | flops 218103808 | bytes 2555904 | tf_op jit(solution)/shard_map/dion_exchange/pallas_call | solution.py:349
  173.4 1.3 fusion.1
  174.7 1.3 fusion.2
Async XLA Ops:
  0.6 1.2 copy-start
  1.8 1.2 copy-start.1
  2.9 0.7 copy-start.2

commit v2 on v0

v2 whole, which is shorter than its diff:
```python
import functools
import math

import jax
import jax.numpy as jnp
from jax import lax
from jax.experimental import pallas as pl
from jax.experimental.pallas import tpu as pltpu
from jax.sharding import PartitionSpec as P

MESH = pl.DeviceIdType.MESH
HIGHEST = lax.Precision.HIGHEST
RANK = 128
NX = 4
NEAR = 8
FAR = 4
CORES = 2
F32 = jnp.float32
BF16 = jnp.bfloat16


class Plan:
    def __init__(self, n_fsdp, n_tensor, rows, cols):
        self.nz, self.nx, self.nt, self.ny = n_fsdp // NX, NX, n_tensor, n_tensor // CORES
        assert self.nz == NEAR * FAR and NX == 4
        self.rows, self.cols = rows, cols
        self.piece = cols // n_fsdp
        self.slot = -(-self.piece // 16) * 16
        self.block = self.piece * FAR
        self.sent = -(-self.block // 16) * 16
        self.group = self.block * NX
        self.near = sorted([d for d in range(-((NEAR - 1) // 2), NEAR // 2 + 1) if d], key=abs)
        self.far = [(2 * i + 1) * (NEAR // 2) for i in range(-(FAR // 2), FAR // 2)]
        self.far.sort(key=abs, reverse=True)
        self.strip = RANK // n_tensor
        self.chunk = 256 if cols % 256 == 0 else cols // self.nx
        self.batches = [(a, b) for a, b in ((0, 1), (1, NEAR // 2 + 1), (NEAR // 2 + 1, NEAR)) if a < b]


class Copies:
    def __init__(self, send, recv):
        self.send, self.recv, self.used, self.out = send, recv, 0, []

    def start(self, src, dst, device):
        i = self.used
        self.used += 1
        copy = pltpu.make_async_remote_copy(
            src_ref=src, dst_ref=dst, send_sem=self.send.at[i], recv_sem=self.recv.at[i],
            device_id=device, device_id_type=MESH,
        )
        copy.start()
        self.out.append(copy)
        return copy

    def drain(self, keep=0):
        n = len(self.out) - keep
        for copy in self.out[:n]:
            copy.wait_send()
        self.out = self.out[n:]


def n_copies(plan):
    near, far, x, y = len(plan.near), len(plan.far), plan.nx - 1, plan.ny - 1
    gather = far + near + x * len(plan.batches)
    return 2 * gather + (y + 2) + (x + near + far + y + 1) + (2 * NEAR + near + far) + (far + near + x + y + 1)


def factor(gp_ref, ot_ref):
    n, nb = RANK, 32
    lane1 = lax.broadcasted_iota(jnp.int32, (1, n), 1)
    for top in range(0, n, nb):
        lane = lax.broadcasted_iota(jnp.int32, (n - top, n), 1)
        row1 = lax.broadcasted_iota(jnp.int32, (n - top, 1), 0) + top

        def step(s, carry, top=top, lane=lane, row1=row1):
            j = top + s * 4
            gram = gp_ref[top:, :n]
            cols, rows = [], []
            for p in range(4):
                rows.append(gp_ref[pl.ds(j + p, 1), :])
                cols.append(jnp.sum(jnp.where(lane == j + p, gram, 0.0), axis=1, keepdims=True))
            a = [[jnp.sum(jnp.where(lane1 == j + q, rows[p][:, :n], 0.0), axis=1, keepdims=True)
                  for q in range(p + 1)] for p in range(4)]
            inv, mults = [], []
            for p in range(4):
                for q in range(p):
                    low = a[p][q] * inv[q]
                    rows[p] = rows[p] - low * rows[q]
                    cols[p] = cols[p] - low * cols[q]
                    for r in range(p, 4):
                        a[r][p] = a[r][p] - low * a[r][q]
                inv.append(1.0 / a[p][p])
                mults.append(jnp.where(row1 > j + 3, cols[p] * inv[p], 0.0))
                ot_ref[pl.ds(j + p, 1), :] = rows[p][:, n:] * (1.0 / jnp.sqrt(a[p][p]))
            new = gp_ref[top:, :]
            for p in range(4):
                new = new - mults[p] * rows[p]
            gp_ref[top:, :] = new
            return carry

        lax.fori_loop(0, nb // 4, step, 0)


def kernel(plan, m_hbm, g_hbm, b_ref, ortho_ref, piece_ref, scale_ref,
           m_ref, g_ref, turned, turned_b, lines, tiles, spread, basis_own, basis_in, packed, basis_buf,
           part, part_c, part_y, panel, strip, gram_x, gram_n, gram_f, gram_t, gp, ot,
           cross, cross_r, cross_x, sum_x, cross_n, sum_n, cross_f, cross_own, cross_held, cross_buf, nat,
           sq, sq_f, sq_n, sq_x, sq_y, sq_c, send_sem, recv_sem, load_sem):
    f, t = lax.axis_index("fsdp"), lax.axis_index("tensor")
    nz, nx, ny = plan.nz, plan.nx, plan.ny
    z, x = f // nx, f % nx
    y, core = t // CORES, t % CORES
    near_id, far_id = z % NEAR, z // NEAR
    comm = Copies(send_sem, recv_sem)

    def at_z(d):
        return (lax.rem(z + d + nz, nz) * nx + x, t)

    x_devices = [(z * nx + lax.rem(x + d, nx), t) for d in (2, 1, 3)]
    y_devices = [(f, lax.rem(y + d, ny) * CORES + core) for d in range(1, ny)]
    sibling = (f, y * CORES + 1 - core)
    right, across, left = (lax.rem(x + d, nx) for d in (1, 2, 3))
    to_right, to_left = x_devices[1], x_devices[2]
    near_devices = [at_z(d) for d in plan.near]
    far_devices = [at_z(d) for d in plan.far]

    loads = [pltpu.make_async_copy(m_hbm, m_ref, load_sem.at[0]), pltpu.make_async_copy(g_hbm, g_ref, load_sem.at[1])]
    for load in loads:
        load.start()
    barrier = pltpu.get_barrier_semaphore()
    peers = far_devices + [at_z(-d) for d in plan.near] + x_devices + y_devices + [sibling]
    for device in peers:
        pl.semaphore_signal(barrier, inc=1, device_id=device, device_id_type=MESH)

    basis_own[...] = jnp.zeros_like(basis_own)
    basis_own[0:plan.piece, :] = b_ref[...].astype(BF16)
    chunk = plan.chunk
    for load in loads:
        load.wait()

    def turn(i, carry):
        c = pl.ds(pl.multiple_of(i * chunk, chunk), chunk)
        value = (m_ref[:, c].astype(F32) + g_ref[:, c].astype(F32)).astype(BF16).astype(F32).T
        turned[c, :] = value
        turned_b[c, :] = value.astype(BF16)
        return carry

    lax.fori_loop(0, plan.cols // chunk, turn, 0)
    tiles[...] = jnp.zeros_like(tiles)
    packed[...] = jnp.zeros_like(packed)
    pl.semaphore_wait(barrier, len(peers))

    def begin(src, slots, devices):
        return [comm.start(src, slots.at[i], device) for i, device in enumerate(devices)]

    def add_up(total, slots, copies):
        for i, copy in enumerate(copies):
            copy.wait_recv()
            total = slots[i] if total is None else total + slots[i]
        return total

    def gathered(near):
        return lax.rem(near_id - near + NEAR + NEAR // 2, NEAR)

    slot = basis_in.at[far_id]
    far_copies = [comm.start(basis_own, slot, device) for device in far_devices]
    piece = plan.piece

    def space(i, carry):
        for k in range(FAR):
            n = nx * piece
            lines[...] = turned[pl.ds(pl.multiple_of((i + NEAR * k) * n, 8), n), :]
            for xx in range(nx):
                tiles[xx, k * piece:(k + 1) * piece, :] = lines[xx * piece:(xx + 1) * piece, :]
        for xx in range(nx):
            spread[xx, i] = tiles[xx].T.astype(BF16)
        return carry

    lax.fori_loop(0, NEAR, space, 0)
    for copy in far_copies:
        copy.wait_recv()
    for k in range(FAR):
        packed[k * piece:(k + 1) * piece, :] = basis_in[k, 0:piece].astype(F32)
    basis_buf[x, 0:plan.sent] = packed[...].astype(BF16)

    shifts = [0] + plan.near

    def pass_on(buf, before_batch=None):
        n = plan.sent
        block = buf.at[x, pl.ds(0, n)]
        z_copies = [comm.start(block, buf.at[x, pl.ds((i + 1) * n, n)], near_devices[i])
                    for i in reversed(range(NEAR - 1))][::-1]
        sent = []
        for a, b in plan.batches:
            for i in range(max(a, 1), b):
                z_copies[i - 1].wait_recv()
            blocks = buf.at[x, pl.ds(a * n, (b - a) * n)]
            sent.append([comm.start(blocks, blocks, device) for device in x_devices])
            if before_batch is not None:
                before_batch(a)
        return sent

    total = jnp.zeros((plan.rows, RANK), F32)
    for (a, b), copies in zip(plan.batches, pass_on(basis_buf)):
        for copy in copies:
            copy.wait_recv()
        for i in range(a, b):
            near = gathered(shifts[i])
            for xx in range(nx):
                total = total + jnp.dot(spread[xx, near][:, :plan.sent],
                                        basis_buf[xx, i * plan.sent:(i + 1) * plan.sent], preferred_element_type=F32)
    part[...] = total

    def half_of(ref, i):
        n = plan.rows // CORES
        return ref.at[pl.ds(pl.multiple_of(i * n, n), n)]

    comm.start(half_of(part, 1 - core), part_c, sibling).wait_recv()
    part_y[y] = half_of(part, core)[...] + part_c[...]
    for copy in [comm.start(part_y.at[y], part_y.at[y], device) for device in y_devices]:
        copy.wait_recv()
    mine = half_of(panel, core)
    total = part_y[0]
    for i in range(1, ny):
        total = total + part_y[i]
    mine[...] = total
    comm.start(mine, mine, sibling).wait_recv()

    w = plan.strip

    def strip_of(ref):
        return ref.at[pl.ds(pl.multiple_of((core * ny + y) * w, w), w)]

    pan = panel[...]
    gp[:, RANK:] = pan.T
    lines_t = gp[pl.ds(pl.multiple_of((core * ny + y) * w, w), w), RANK:]
    strip[0] = jnp.dot(lines_t, pan, precision=HIGHEST, preferred_element_type=F32)
    strip[1] = add_up(strip[0], gram_x, begin(strip.at[0], gram_x, x_devices))
    strip[2] = add_up(strip[1], gram_n, begin(strip.at[1], gram_n, near_devices[::-1]))
    copies = begin(strip.at[2], gram_f, far_devices)
    comm.drain(keep=FAR)
    mine = strip_of(gram_t)
    mine[...] = add_up(None, gram_f, copies)
    for copy in [comm.start(mine, mine, device) for device in y_devices]:
        copy.wait_recv()
    mine = half_of(gram_t, core)
    comm.start(mine, mine, sibling).wait_recv()
    gp[:, :RANK] = gram_t[...]

    factor(gp, ot)
    ortho = ot[...].T.astype(BF16)
    ortho_ref[...] = ortho

    rows, group = plan.block, plan.group
    order = plan.near[::-1] + [0]
    pairs = [(o, o + 1) for o in range(0, NEAR, 2)]
    z_copies = []
    sum_n[...] = jnp.zeros_like(sum_n)

    def send_x(pair):
        for o in pair:
            first = lax.rem(near_id + order[o] + NEAR + NEAR // 2, NEAR) * group
            value = jnp.dot(turned_b[pl.ds(pl.multiple_of(first, 16), group), :], ortho, preferred_element_type=F32)
            for xx in range(nx):
                cross[xx, o] = value[xx * rows:(xx + 1) * rows, :]
        a, b = pair
        return [comm.start(cross.at[across, a], cross_r.at[0, a], to_right),
                comm.start(cross.at[across, b], cross_r.at[1, a], to_left)]

    def pass_x(pair, copies):
        a, b = pair
        for copy in copies:
            copy.wait_recv()
        cross[right, a] += cross_r[0, a]
        cross[left, b] += cross_r[1, a]
        return [comm.start(cross.at[xx, pl.ds(a, 2)], cross_x.at[i, pl.ds(a, 2)], device)
                for i, (xx, device) in enumerate(((right, to_right), (left, to_left)))]

    def add_x(pair, copies):
        for copy in copies:
            copy.wait_recv()
        for o in pair:
            total = cross[x, o] + cross_x[0, o] + cross_x[1, o]
            if order[o]:
                sum_x[o] = total
                z_copies.append(comm.start(sum_x.at[o], cross_n.at[o], at_z(order[o])))
            else:
                sum_n[0:rows, :] = add_up(total, cross_n, z_copies)

    first, second = [], []
    for i in range(len(pairs) + 2):
        if i < len(pairs):
            first.append(send_x(pairs[i]))
        if 1 <= i <= len(pairs):
            second.append(pass_x(pairs[i - 1], first[i - 1]))
        if i >= 2:
            add_x(pairs[i - 2], second[i - 2])

    def far_rows(i):
        return pl.ds(pl.multiple_of(i * plan.slot, plan.slot), plan.slot)

    copies = [comm.start(sum_n.at[far_rows(lax.rem(z + d + nz, nz) // NEAR)], cross_f.at[i], device)
              for i, (d, device) in enumerate(zip(plan.far, far_devices))]
    comm.drain(keep=FAR)
    total = add_up(None, cross_f, copies)

    cross_own[...] = total.astype(BF16)
    slot = cross_held.at[far_rows(far_id)]
    far_copies = [comm.start(cross_own, slot, device) for device in far_devices]
    sq[0] = jnp.broadcast_to(jnp.sum(total * total, axis=0, keepdims=True), (8, RANK))
    sq_copies = begin(sq.at[0], sq_f, far_devices)
    comm.drain(keep=2 * FAR)
    for copy in far_copies:
        copy.wait_recv()
    cross_buf[x, 0:plan.sent] = cross_held[0:plan.sent, :]
    sq[1] = add_up(None, sq_f, sq_copies)
    sq_copies = begin(sq.at[1], sq_n, near_devices)

    def before_batch(a):
        if a == 0:
            sq[2] = add_up(sq[1], sq_n, sq_copies)
            later.append(begin(sq.at[2], sq_x, x_devices))

    later = []
    batches = list(zip(plan.batches, pass_on(cross_buf, before_batch)))
    sq[3] = add_up(sq[2], sq_x, later[0])
    sq_copies = begin(sq.at[3], sq_y, y_devices)

    def settle(batch):
        (a, b), copies = batch
        for copy in copies:
            copy.wait_recv()
        for i in range(a, b):
            for xx in range(nx):
                nat[xx * rows:(xx + 1) * rows, :] = cross_buf[xx, i * plan.sent:i * plan.sent + rows].astype(F32)
            first = pl.multiple_of(gathered(shifts[i]) * group, 16)
            piece_ref[pl.ds(first, group), :] = nat[...].astype(BF16)

    for batch in batches[:-1]:
        settle(batch)
    sq[4] = add_up(sq[3], sq_y, sq_copies)
    last = comm.start(sq.at[4], sq_c.at[0], sibling)
    settle(batches[-1])
    scale_ref[...] = 1.0 / jnp.sqrt(add_up(sq[4], sq_c, [last]) + 1e-06)
    comm.drain()


def exchange(plan, momentum, gradient, basis):
    nx, ny, near, far = plan.nx, plan.ny, len(plan.near), len(plan.far)
    w, half = plan.strip, plan.rows // CORES

    def f32(*shape):
        return pltpu.VMEM((*shape, RANK), F32)

    def bf16(*shape):
        return pltpu.VMEM((*shape, RANK), BF16)

    whole = pltpu.VMEM((plan.rows, plan.cols), BF16)
    scratch = [
        whole, whole, f32(plan.cols), bf16(plan.cols), f32(nx * plan.piece), f32(nx, FAR * plan.slot),
        pltpu.VMEM((nx, NEAR, plan.rows, FAR * plan.slot), BF16), bf16(plan.slot), bf16(FAR, plan.slot),
        f32(plan.sent), bf16(nx, NEAR * plan.sent),
        f32(plan.rows), f32(half), f32(ny, half), f32(plan.rows), f32(3, w),
        f32(nx - 1, w), f32(near, w), f32(far, w), f32(RANK),
        pltpu.VMEM((RANK, RANK + plan.rows), F32), pltpu.VMEM((RANK, plan.rows), F32),
        f32(nx, NEAR, plan.block), f32(2, NEAR, plan.block), f32(2, NEAR, plan.block), f32(near, plan.block), f32(near, plan.block),
        f32(FAR * plan.slot), f32(far, plan.slot), bf16(plan.slot), bf16(FAR * plan.slot), bf16(nx, NEAR * plan.sent),
        f32(plan.group),
        f32(5, 8), f32(far, 8), f32(near, 8), f32(nx - 1, 8), f32(max(ny - 1, 1), 8), f32(1, 8),
        pltpu.SemaphoreType.DMA((n_copies(plan),)),
        pltpu.SemaphoreType.DMA((n_copies(plan),)),
        pltpu.SemaphoreType.DMA((2,)),
    ]
    vmem, hbm = pl.BlockSpec(memory_space=pltpu.VMEM), pl.BlockSpec(memory_space=pl.ANY)
    return pl.pallas_call(
        functools.partial(kernel, plan),
        out_shape=(
            jax.ShapeDtypeStruct((plan.rows, RANK), BF16),
            jax.ShapeDtypeStruct((plan.cols, RANK), BF16),
            jax.ShapeDtypeStruct((8, RANK), F32),
        ),
        in_specs=[hbm, hbm, vmem],
        out_specs=(vmem,) * 3,
        scratch_shapes=scratch,
        compiler_params=pltpu.CompilerParams(
            collective_id=0, has_side_effects=True, vmem_limit_bytes=56 * 1024 * 1024),
        cost_estimate=pl.CostEstimate(
            flops=4 * plan.rows * plan.cols * RANK, bytes_accessed=6 * plan.rows * plan.cols, transcendentals=0),
        name="dion_exchange",
    )(momentum, gradient, basis)


def solution(mesh):
    n_fsdp, n_tensor = mesh.shape["fsdp"], mesh.shape["tensor"]

    def body(momentum, gradient, basis):
        rows, cols = momentum.shape
        plan = Plan(n_fsdp, n_tensor, rows, cols)
        scale = math.sqrt(rows * n_fsdp * cols * n_tensor / RANK)
        ortho, piece, scaleinv = exchange(plan, momentum, gradient, basis)
        newbasis = (piece.astype(F32) * scaleinv[0:1]).astype(BF16)
        dims = (((1,), (1,)), ((), ()))
        update = scale * lax.dot_general(ortho, newbasis, dims, preferred_element_type=F32)
        summed = momentum.astype(F32) + gradient.astype(F32)
        moved = summed - 0.05 * lax.dot_general(ortho, piece, dims, preferred_element_type=F32)
        return update.astype(BF16), moved.astype(BF16)

    in_specs = (P("fsdp", "tensor"), P("fsdp", "tensor"), P(("tensor", "fsdp"), None))
    out_specs = (P("fsdp", "tensor"), P("fsdp", "tensor"))
    return jax.shard_map(body, mesh=mesh, in_specs=in_specs, out_specs=out_specs, check_vma=False)
```

time: 1600 us -> 157 us (0.10)
  the two profiles are of different devices: /device:TPU:2 before, /device:TPU:1 now
where the time goes in v2:
time: 157 us
  Pallas kernels  152 us (97%)
  matrix products  3.96 us (3%)
    pallas_call x1, Pallas kernels, exchange(): pl.pallas_call(functools.partial(kernel, plan), out_shape=(jax.ShapeDtype...  152 us

profile of v2, /device:TPU:1, one launch (start us, length us, event | category | flops | bytes accessed | tf_op | source)
XLA Modules:
  0.0 157.1 jit_solution(17014270121272201307)
XLA Ops:
  0.6 0.0 copy-start.2
  0.6 151.8 %dion_exchange.1 = (bf16[128,128]{1,0:T(8,128)(2,1)}, bf16[3328,128]{1,0:T(8,128)(2,1)}, f32[8,128]{1,0:T(8,128)}) custom-call(bf16[128,3328]{1,0:T(8,128)(2,1)} %m_hbm.1, bf16[128,3328]{1,0:T(8,128)(2,1)} %g_hbm.1, f32[26,128]{1,0:T(8,128)} %b_ref.1), custom_call_target="tpu_custom_call" | custom-call | flops 218103808 | bytes 2555904 | tf_op jit(solution)/shard_map/dion_exchange/pallas_call | solution.py:375
  152.5 0.7 slice_bitcast_fusion
  153.1 0.0 copy-start
  153.1 0.0 copy-start.1
  153.1 0.0 copy-start.3
  153.1 2.6 %fusion.1 = bf16[128,3328]{1,0:T(8,128)(2,1)} fusion(bf16[128,128]{1,0:T(8,128)(2,1)} %get-tuple-element.5, bf16[3328,128]{1,0:T(8,128)(2,1)} %get-tuple-element.6, f32[128]{0:T(128)S(1)} %slice_bitcast_fusion), kind=kOutput, calls=%fused_computation.3 | convolution fusion | flops 111181824 | bytes 1737216 | tf_op jit(solution)/shard_map/dot_general | solution.py:403
  155.7 0.0 copy-done.2
  155.7 0.0 copy-done
  155.7 0.0 copy-done.1
  155.8 0.0 copy-done.3
  155.8 1.4 fusion.2
Async XLA Ops:
  0.6 155.1 %copy-start.2 = (bf16[128,3328]{1,0:T(8,128)(2,1)S(1)}, bf16[128,3328]{1,0:T(8,128)(2,1)}, u32[]{:S(2)}) copy-start(bf16[128,3328]{1,0:T(8,128)(2,1)} %g_hbm.1) | copy-start | bytes 2555908
  153.1 2.6 %copy-start = (bf16[3328,128]{1,0:T(8,128)(2,1)S(1)}, bf16[3328,128]{1,0:T(8,128)(2,1)}, u32[]{:S(2)}) copy-start(bf16[3328,128]{1,0:T(8,128)(2,1)} %get-tuple-element.6) | copy-start | bytes 2555908
  153.1 2.6 %copy-start.1 = (bf16[128,3328]{1,0:T(8,128)(2,1)S(1)}, bf16[128,3328]{1,0:T(8,128)(2,1)}, u32[]{:S(2)}) copy-start(bf16[128,3328]{1,0:T(8,128)(2,1)} %m_hbm.1) | copy-start | bytes 2555908
  153.1 2.6 %copy-start.3 = (bf16[128,128]{1,0:T(8,128)(2,1)S(1)}, bf16[128,128]{1,0:T(8,128)(2,1)}, u32[]{:S(2)}) copy-start(bf16[128,128]{1,0:T(8,128)(2,1)} %get-tuple-element.5) | copy-start | bytes 98308

commit v3 on v2

--- a/solution.py
+++ b/solution.py
@@ -34,7 +34,8 @@
         self.far.sort(key=abs, reverse=True)
         self.strip = RANK // n_tensor
         self.chunk = 256 if cols % 256 == 0 else cols // self.nx
-        self.batches = [(a, b) for a, b in ((0, 1), (1, NEAR // 2 + 1), (NEAR // 2 + 1, NEAR)) if a < b]
+        edges = [0] + [e for e in (1, 3, 5) if e < NEAR] + [NEAR]
+        self.batches = list(zip(edges, edges[1:]))
 
 
 class Copies:
@@ -62,7 +63,7 @@
 def n_copies(plan):
     near, far, x, y = len(plan.near), len(plan.far), plan.nx - 1, plan.ny - 1
     gather = far + near + x * len(plan.batches)
-    return 2 * gather + (y + 2) + (x + near + far + y + 1) + (2 * NEAR + near + far) + (far + near + x + y + 1)
+    return 2 * gather + (y + 2) + (2 * x + 1 + near + far + y + 1) + (2 * NEAR + near + far) + (far + near + x + y + 1)
 
 
 def factor(gp_ref, ot_ref):
@@ -103,7 +104,7 @@
 
 def kernel(plan, m_hbm, g_hbm, b_ref, ortho_ref, piece_ref, scale_ref,
            m_ref, g_ref, turned, turned_b, lines, tiles, spread, basis_own, basis_in, packed, basis_buf,
-           part, part_c, part_y, panel, strip, gram_x, gram_n, gram_f, gram_t, gp, ot,
+           part, part_c, part_y, panel, half_t, halves, strip, gram_x, gram_n, gram_f, gram_t, gp, ot,
            cross, cross_r, cross_x, sum_x, cross_n, sum_n, cross_f, cross_own, cross_held, cross_buf, nat,
            sq, sq_f, sq_n, sq_x, sq_y, sq_c, send_sem, recv_sem, load_sem):
     f, t = lax.axis_index("fsdp"), lax.axis_index("tensor")
@@ -119,6 +120,7 @@
     x_devices = [(z * nx + lax.rem(x + d, nx), t) for d in (2, 1, 3)]
     y_devices = [(f, lax.rem(y + d, ny) * CORES + core) for d in range(1, ny)]
     sibling = (f, y * CORES + 1 - core)
+    other_devices = [(device[0], sibling[1]) for device in x_devices]
     right, across, left = (lax.rem(x + d, nx) for d in (1, 2, 3))
     to_right, to_left = x_devices[1], x_devices[2]
     near_devices = [at_z(d) for d in plan.near]
@@ -128,7 +130,7 @@
     for load in loads:
         load.start()
     barrier = pltpu.get_barrier_semaphore()
-    peers = far_devices + [at_z(-d) for d in plan.near] + x_devices + y_devices + [sibling]
+    peers = far_devices + [at_z(-d) for d in plan.near] + x_devices + y_devices + [sibling] + other_devices
     for device in peers:
         pl.semaphore_signal(barrier, inc=1, device_id=device, device_id_type=MESH)
 
@@ -185,19 +187,19 @@
 
     shifts = [0] + plan.near
 
-    def pass_on(buf, before_batch=None):
+    def pass_on(buf, after_batch=None):
         n = plan.sent
         block = buf.at[x, pl.ds(0, n)]
         z_copies = [comm.start(block, buf.at[x, pl.ds((i + 1) * n, n)], near_devices[i])
-                    for i in reversed(range(NEAR - 1))][::-1]
+                    for i in range(NEAR - 1)]
         sent = []
         for a, b in plan.batches:
             for i in range(max(a, 1), b):
                 z_copies[i - 1].wait_recv()
             blocks = buf.at[x, pl.ds(a * n, (b - a) * n)]
             sent.append([comm.start(blocks, blocks, device) for device in x_devices])
-            if before_batch is not None:
-                before_batch(a)
+            if after_batch is not None:
+                after_batch(a)
         return sent
 
     total = jnp.zeros((plan.rows, RANK), F32)
@@ -224,22 +226,26 @@
     for i in range(1, ny):
         total = total + part_y[i]
     mine[...] = total
-    comm.start(mine, mine, sibling).wait_recv()
+    half_copy = comm.start(mine, mine, sibling)
 
     w = plan.strip
 
-    def strip_of(ref):
-        return ref.at[pl.ds(pl.multiple_of((core * ny + y) * w, w), w)]
-
-    pan = panel[...]
-    gp[:, RANK:] = pan.T
-    lines_t = gp[pl.ds(pl.multiple_of((core * ny + y) * w, w), w), RANK:]
-    strip[0] = jnp.dot(lines_t, pan, precision=HIGHEST, preferred_element_type=F32)
-    strip[1] = add_up(strip[0], gram_x, begin(strip.at[0], gram_x, x_devices))
+    def strip_rows(i):
+        return pl.ds(pl.multiple_of((i * ny + y) * w, w), w)
+
+    half_t[...] = total.T
+    for i in range(CORES):
+        halves[i] = jnp.dot(half_t[strip_rows(i), :], total, precision=HIGHEST, preferred_element_type=F32)
+    copies = [comm.start(halves.at[1 - core], gram_x.at[i], device)
+              for i, device in enumerate(other_devices + [sibling])]
+    copies += [comm.start(halves.at[core], gram_x.at[i + nx], device) for i, device in enumerate(x_devices)]
+    strip[1] = add_up(halves[core], gram_x, copies)
     strip[2] = add_up(strip[1], gram_n, begin(strip.at[1], gram_n, near_devices[::-1]))
     copies = begin(strip.at[2], gram_f, far_devices)
+    half_copy.wait_recv()
+    gp[:, RANK:] = panel[...].T
     comm.drain(keep=FAR)
-    mine = strip_of(gram_t)
+    mine = gram_t.at[strip_rows(core)]
     mine[...] = add_up(None, gram_f, copies)
     for copy in [comm.start(mine, mine, device) for device in y_devices]:
         copy.wait_recv()
@@ -313,17 +319,18 @@
     for copy in far_copies:
         copy.wait_recv()
     cross_buf[x, 0:plan.sent] = cross_held[0:plan.sent, :]
-    sq[1] = add_up(None, sq_f, sq_copies)
-    sq_copies = begin(sq.at[1], sq_n, near_devices)
-
-    def before_batch(a):
+
+    def after_batch(a):
         if a == 0:
-            sq[2] = add_up(sq[1], sq_n, sq_copies)
+            sq[1] = add_up(None, sq_f, sq_copies)
+            later.append(begin(sq.at[1], sq_n, near_devices))
+        if a == 1:
+            sq[2] = add_up(sq[1], sq_n, later[0])
             later.append(begin(sq.at[2], sq_x, x_devices))
 
     later = []
-    batches = list(zip(plan.batches, pass_on(cross_buf, before_batch)))
-    sq[3] = add_up(sq[2], sq_x, later[0])
+    batches = list(zip(plan.batches, pass_on(cross_buf, after_batch)))
+    sq[3] = add_up(sq[2], sq_x, later[1])
     sq_copies = begin(sq.at[3], sq_y, y_devices)
 
     def settle(batch):
@@ -341,7 +348,7 @@
     sq[4] = add_up(sq[3], sq_y, sq_copies)
     last = comm.start(sq.at[4], sq_c.at[0], sibling)
     settle(batches[-1])
-    scale_ref[...] = 1.0 / jnp.sqrt(add_up(sq[4], sq_c, [last]) + 1e-06)
+    scale_ref[...] = 1.0 / jnp.sqrt(add_up(sq[4], sq_c, [last])[0:1, :] + 1e-06)
     comm.drain()
 
 
@@ -360,8 +367,8 @@
         whole, whole, f32(plan.cols), bf16(plan.cols), f32(nx * plan.piece), f32(nx, FAR * plan.slot),
         pltpu.VMEM((nx, NEAR, plan.rows, FAR * plan.slot), BF16), bf16(plan.slot), bf16(FAR, plan.slot),
         f32(plan.sent), bf16(nx, NEAR * plan.sent),
-        f32(plan.rows), f32(half), f32(ny, half), f32(plan.rows), f32(3, w),
-        f32(nx - 1, w), f32(near, w), f32(far, w), f32(RANK),
+        f32(plan.rows), f32(half), f32(ny, half), f32(plan.rows),
+        pltpu.VMEM((RANK, half), F32), f32(CORES, w), f32(3, w), f32(2 * nx - 1, w), f32(near, w), f32(far, w), f32(RANK),
         pltpu.VMEM((RANK, RANK + plan.rows), F32), pltpu.VMEM((RANK, plan.rows), F32),
         f32(nx, NEAR, plan.block), f32(2, NEAR, plan.block), f32(2, NEAR, plan.block), f32(near, plan.block), f32(near, plan.block),
         f32(FAR * plan.slot), f32(far, plan.slot), bf16(plan.slot), bf16(FAR * plan.slot), bf16(nx, NEAR * plan.sent),
@@ -377,7 +384,7 @@
         out_shape=(
             jax.ShapeDtypeStruct((plan.rows, RANK), BF16),
             jax.ShapeDtypeStruct((plan.cols, RANK), BF16),
-            jax.ShapeDtypeStruct((8, RANK), F32),
+            jax.ShapeDtypeStruct((1, RANK), F32),
         ),
         in_specs=[hbm, hbm, vmem],
         out_specs=(vmem,) * 3,
@@ -390,6 +397,41 @@
     )(momentum, gradient, basis)
 
 
+def write(scale, m_ref, g_ref, ortho_ref, piece_ref, scale_ref, update_ref, moved_ref):
+    ortho, scaleinv = ortho_ref[...], scale_ref[...]
+    n = 128 if piece_ref.shape[0] % 128 == 0 else piece_ref.shape[0]
+    dims = (((1,), (1,)), ((), ()))
+    for i in range(0, piece_ref.shape[0], n):
+        c = slice(i, i + n)
+        piece = piece_ref[c, :]
+        newbasis = (piece.astype(F32) * scaleinv).astype(BF16)
+        update = scale * lax.dot_general(ortho, newbasis, dims, preferred_element_type=F32)
+        update_ref[:, c] = update.astype(BF16)
+        summed = m_ref[:, c].astype(F32) + g_ref[:, c].astype(F32)
+        moved = summed - 0.05 * lax.dot_general(ortho, piece, dims, preferred_element_type=F32)
+        moved_ref[:, c] = moved.astype(BF16)
+
+
+def outputs(scale, momentum, gradient, ortho, piece, scaleinv):
+    rows, cols = momentum.shape
+    steps = 2 if cols % 256 == 0 else 1
+    wide = pl.BlockSpec((rows, cols // steps), lambda i: (0, i))
+    return pl.pallas_call(
+        functools.partial(write, scale),
+        out_shape=(jax.ShapeDtypeStruct((rows, cols), BF16),) * 2,
+        grid=(steps,),
+        in_specs=[
+            wide, wide, pl.BlockSpec((rows, RANK), lambda i: (0, 0)),
+            pl.BlockSpec((cols // steps, RANK), lambda i: (i, 0)), pl.BlockSpec((1, RANK), lambda i: (0, 0)),
+        ],
+        out_specs=(wide, wide),
+        compiler_params=pltpu.CompilerParams(vmem_limit_bytes=32 * 1024 * 1024),
+        cost_estimate=pl.CostEstimate(
+            flops=4 * rows * cols * RANK, bytes_accessed=8 * rows * cols + 2 * cols * RANK, transcendentals=0),
+        name="dion_outputs",
+    )(momentum, gradient, ortho, piece, scaleinv)
+
+
 def solution(mesh):
     n_fsdp, n_tensor = mesh.shape["fsdp"], mesh.shape["tensor"]
 
@@ -398,12 +440,7 @@
         plan = Plan(n_fsdp, n_tensor, rows, cols)
         scale = math.sqrt(rows * n_fsdp * cols * n_tensor / RANK)
         ortho, piece, scaleinv = exchange(plan, momentum, gradient, basis)
-        newbasis = (piece.astype(F32) * scaleinv[0:1]).astype(BF16)
-        dims = (((1,), (1,)), ((), ()))
-        update = scale * lax.dot_general(ortho, newbasis, dims, preferred_element_type=F32)
-        summed = momentum.astype(F32) + gradient.astype(F32)
-        moved = summed - 0.05 * lax.dot_general(ortho, piece, dims, preferred_element_type=F32)
-        return update.astype(BF16), moved.astype(BF16)
+        return outputs(scale, momentum, gradient, ortho, piece, scaleinv)
 
     in_specs = (P("fsdp", "tensor"), P("fsdp", "tensor"), P(("tensor", "fsdp"), None))
     out_specs = (P("fsdp", "tensor"), P("fsdp", "tensor"))

time: 157 us -> 155 us (0.987)
  matrix products: 3.96 us -> 0 us
  local copies, waits for them, and re-layouts: 0.69 us -> 2.56 us
    dot_general x2 -> x0, matrix products: 3.96 us -> none  [the longest x1 2.6 us: body(): lax.dot_general(ortho, newbasis, dims, preferred_element_type=F32)]
    pallas_call x1, Pallas kernels: 152 us -> 149 us  [exchange(): pl.pallas_call(functools.partial(kernel, plan), out_shape=(jax.ShapeDtype...]
    unnamed x8 -> x10, local copies, waits for them, and re-layouts: 0.02 us -> 2.56 us
    pallas_call x0 -> x1, Pallas kernels: none -> 2.48 us  [outputs(): pl.pallas_call(functools.partial(write, scale), out_shape=(jax.ShapeDtype...]
where the time goes in v3:
time: 155 us
  Pallas kernels  152 us (98%)
  local copies, waits for them, and re-layouts  2.56 us (2%)
    pallas_call x1, Pallas kernels, exchange(): pl.pallas_call(functools.partial(kernel, plan), out_shape=(jax.ShapeDtype...  149 us

profile of v3, /device:TPU:1, one launch (start us, length us, event | category | flops | bytes accessed | tf_op | source)
XLA Modules:
  0.0 154.9 jit_solution(13908073961447567048)
XLA Ops:
  0.6 0.0 copy-start.1
  0.6 0.0 copy-start
  0.6 149.2 %dion_exchange.1 = (bf16[128,128]{1,0:T(8,128)(2,1)}, bf16[3328,128]{1,0:T(8,128)(2,1)}, f32[1,128]{1,0:T(1,128)}) custom-call(bf16[128,3328]{1,0:T(8,128)(2,1)} %m_ref.1, bf16[128,3328]{1,0:T(8,128)(2,1)} %g_ref.1, f32[26,128]{1,0:T(8,128)} %b_ref.1), custom_call_target="tpu_custom_call" | custom-call | flops 218103808 | bytes 2555904 | tf_op jit(solution)/shard_map/dion_exchange/pallas_call | solution.py:382
  149.9 0.0 copy-start.4
  149.9 0.0 copy-done.1
  149.9 0.0 copy-done
  149.9 0.6 copy-done.4
  150.5 0.0 copy-start.2
  150.5 1.2 copy-done.2
  151.7 0.0 copy-start.3
  151.7 0.8 copy-done.3
  152.5 2.5 %dion_outputs.1 = (bf16[128,3328]{1,0:T(8,128)(2,1)}, bf16[128,3328]{1,0:T(8,128)(2,1)}) custom-call(bf16[128,3328]{1,0:T(8,128)(2,1)S(1)} %copy-done, bf16[128,3328]{1,0:T(8,128)(2,1)S(1)} %copy-done.1, bf16[128,128]{1,0:T(8,128)(2,1)S(1)} %copy-done.3, bf16[3328,128]{1,0:T(8,128)(2,1)S(1)} %copy-done.2, f32[1,128]{1,0:T(1,128)S(1)} %copy-done.4), custom_call_target="tpu_custom_call" | custom-call | flops 218103808 | bytes 4259840 | tf_op jit(solution)/shard_map/dion_outputs/pallas_call | solution.py:419
Async XLA Ops:
  0.6 149.3 %copy-start.1 = (bf16[128,3328]{1,0:T(8,128)(2,1)S(1)}, bf16[128,3328]{1,0:T(8,128)(2,1)}, u32[]{:S(2)}) copy-start(bf16[128,3328]{1,0:T(8,128)(2,1)} %g_ref.1) | copy-start | bytes 2555908
  0.6 149.3 %copy-start = (bf16[128,3328]{1,0:T(8,128)(2,1)S(1)}, bf16[128,3328]{1,0:T(8,128)(2,1)}, u32[]{:S(2)}) copy-start(bf16[128,3328]{1,0:T(8,128)(2,1)} %m_ref.1) | copy-start | bytes 2555908
  149.9 0.7 copy-start.4
  150.5 1.2 copy-start.2
  151.7 0.8 copy-start.3

commit v4 on v3

--- a/solution.py
+++ b/solution.py
@@ -425,7 +425,7 @@
             pl.BlockSpec((cols // steps, RANK), lambda i: (i, 0)), pl.BlockSpec((1, RANK), lambda i: (0, 0)),
         ],
         out_specs=(wide, wide),
-        compiler_params=pltpu.CompilerParams(vmem_limit_bytes=32 * 1024 * 1024),
+        compiler_params=pltpu.CompilerParams(vmem_limit_bytes=63 * 1024 * 1024),
         cost_estimate=pl.CostEstimate(
             flops=4 * rows * cols * RANK, bytes_accessed=8 * rows * cols + 2 * cols * RANK, transcendentals=0),
         name="dion_outputs",

time: 155 us -> 154 us (level)
  local copies, waits for them, and re-layouts: 2.56 us -> 0 us
    unnamed x10 -> x0, local copies, waits for them, and re-layouts: 2.56 us -> none
where the time goes in v4:
time: 154 us; the launch traced here: 153 us
  Pallas kernels  153 us (99%)
    pallas_call x1, Pallas kernels, exchange(): pl.pallas_call(functools.partial(kernel, plan), out_shape=(jax.ShapeDtype...  149 us
    pallas_call x1, Pallas kernels, outputs(): pl.pallas_call(functools.partial(write, scale), out_shape=(jax.ShapeDtype...  3.65 us

profile of v4, /device:TPU:1, one launch (start us, length us, event | category | flops | bytes accessed | tf_op | source)
XLA Modules:
  0.0 153.4 jit_solution(2517548170789405469)
XLA Ops:
  0.6 149.1 %dion_exchange.1 = (bf16[128,128]{1,0:T(8,128)(2,1)}, bf16[3328,128]{1,0:T(8,128)(2,1)}, f32[1,128]{1,0:T(1,128)}) custom-call(bf16[128,3328]{1,0:T(8,128)(2,1)} %m_ref.1, bf16[128,3328]{1,0:T(8,128)(2,1)} %g_ref.1, f32[26,128]{1,0:T(8,128)} %b_ref.1), custom_call_target="tpu_custom_call" | custom-call | flops 218103808 | bytes 2555904 | tf_op jit(solution)/shard_map/dion_exchange/pallas_call | solution.py:382
  149.7 3.6 %dion_outputs.1 = (bf16[128,3328]{1,0:T(8,128)(2,1)}, bf16[128,3328]{1,0:T(8,128)(2,1)}) custom-call(bf16[128,3328]{1,0:T(8,128)(2,1)} %m_ref.1, bf16[128,3328]{1,0:T(8,128)(2,1)} %g_ref.1, bf16[128,128]{1,0:T(8,128)(2,1)} %get-tuple-element.5.ortho_ref, bf16[3328,128]{1,0:T(8,128)(2,1)} %get-tuple-element.6.piece_ref, f32[1,128]{1,0:T(1,128)} %get-tuple-element.7.scale_ref), custom_call_target="tpu_custom_call" | custom-call | flops 218103808 | bytes 4259840 | tf_op jit(solution)/shard_map/dion_outputs/pallas_call | solution.py:419
